TPU v7x, 1024 devices: a whole 8x8x8 slice. The times are simulated.
1024 devices in a mesh: gx: 64 (over y, x), gy: 16 (over z, core).
Axes of the slice: x: 8, y: 8, z: 8, core: 2. Of those that a mesh axis runs over, the one named last changes fastest.
Arguments:
- water_depth: float32 [512, 16384], P('gx', 'gy'), may hold values from 0 to 2
- velocity: float32 [2, 512, 16384], P(None, 'gx', 'gy'), may hold values from -1.2 to 1.2
- bathymetry: float32 [512, 16384], P('gx', 'gy'), may hold values from -0.5 to 0.5
- wet_tiles: int32 [64, 128], P('gx', 'gy'), may hold values from 0 to 1, as said below
- migration: int32 [64, 128], P('gx', 'gy'), may hold values from 0 to 15, as said below
Outputs:
- final_state: float32 [3, 512, 16384], P(None, 'gx', 'gy')
Inputs may be any that keep to these rules, and one draw needn't show every extreme that they name: `wet_tiles`: after the tiles move, every device holds exactly 4 wet tiles. `migration`: the 8 tiles of one device go to distinct devices of its row of tiles (itself possibly among them), and every device receives exactly one tile for each value of t mod 8.
All inputs are finite; a program needn't handle non-finite values.
Results may differ from a plain program's by a relative error of at most 0.0003.
Values sent between devices are 32-bit elements; how exact they have to be, the bound alone decides.
A program may use at most 32 MiB of HBM per device.

v0:
```python
import functools

import jax
import jax.numpy as jnp
from jax import lax
from jax.experimental import pallas as pl
from jax.experimental.pallas import tpu as pltpu
from jax.sharding import PartitionSpec as P

DRY_DEPTH = 0.05
COURANT = 0.15
HALO = 4
ROWS = 8
LANES = 128
REACH = 8
WET_LANE = 32
MESH = pl.DeviceIdType.MESH
CORNERS = ((0, 0), (1, 0), (0, 1), (1, 1))


def lanes_of(shape):
    return lax.broadcasted_iota(jnp.int32, shape, len(shape) - 1)


def turn(x, by, axis):
    return pltpu.roll(x, by % x.shape[axis], axis)


def ring_next(tiles):
    turned = [turn(x, -1, 1) for x in tiles]
    last = lanes_of(turned[0].shape) == LANES - 1
    return [jnp.where(last, turned[(c + 1) % len(tiles)], turned[c]) for c in range(len(tiles))]


def ring_previous(tiles):
    turned = [turn(x, 1, 1) for x in tiles]
    first = lanes_of(turned[0].shape) == 0
    return [jnp.where(first, turned[c - 1], turned[c]) for c in range(len(tiles))]


def rates(state):
    parts = []
    for h, p, q in state:
        floored = jnp.maximum(h, DRY_DEPTH)
        inverse_root = lax.rsqrt(floored)
        celerity = floored * inverse_root
        inverse = inverse_root * inverse_root
        u = p * inverse
        v = q * inverse
        pressure = 0.5 * h * h
        parts.append(
            (h, p, q, p * u + pressure, q * u, q * v + pressure, jnp.abs(u) + celerity, jnp.abs(v) + celerity)
        )
    fields = list(zip(*parts))
    h, p, q, east, cross, north, reach_x, reach_y = fields
    on = [ring_next(x) for x in (h, p, q, east, cross, reach_x)]
    faces = [[], [], []]
    for c in range(len(state)):
        wave = jnp.maximum(reach_x[c], on[5][c])
        faces[0].append(p[c] + on[1][c] - wave * (on[0][c] - h[c]))
        faces[1].append(east[c] + on[3][c] - wave * (on[1][c] - p[c]))
        faces[2].append(cross[c] + on[4][c] - wave * (on[2][c] - q[c]))
    back = [ring_previous(x) for x in faces]
    out = []
    for c in range(len(state)):
        below = [turn(x[c], -1, 0) for x in (h, p, q, cross, north, reach_y)]
        wave = jnp.maximum(reach_y[c], below[5])
        rows = (
            q[c] + below[2] - wave * (below[0] - h[c]),
            cross[c] + below[3] - wave * (below[1] - p[c]),
            north[c] + below[4] - wave * (below[2] - q[c]),
        )
        out.append(
            tuple((faces[f][c] - back[f][c]) + (rows[f] - turn(rows[f], 1, 0)) for f in range(3))
        )
    return out


def half_step(state, slopes, masks, start):
    out = []
    changes = rates(state)
    for c, (cells, change, slope, mask) in enumerate(zip(state, changes, slopes, masks)):
        moved = [cells[0] - (0.5 * COURANT) * change[0]]
        for f in (1, 2):
            moved.append(cells[f] - (0.5 * COURANT) * change[f] - cells[0] * slope[f - 1])
        if start is not None:
            moved = [0.5 * start[c][f] + 0.5 * moved[f] for f in range(3)]
        out.append(tuple(x * mask for x in moved))
    return out


def two_steps(state, slopes, masks):
    for _ in range(2):
        middle = half_step(state, slopes, masks, None)
        state = half_step(middle, slopes, masks, state)
    return state


def kernel(
    sizes,
    depth_hbm,
    velocity_hbm,
    bed_hbm,
    wet_hbm,
    migration_hbm,
    out_ref,
    own,
    above,
    below,
    strip,
    strips,
    corners,
    wet,
    migration,
    homes,
    homes_flat,
    tiles,
    outgoing,
    arrived,
    load_sem,
    flat_sem,
    halo_send,
    halo_recv,
    strip_send,
    strip_recv,
    corner_send,
    corner_recv,
    home_send,
    home_recv,
    slot_send,
    slot_recv,
):
    n_rows, n_cols = sizes
    tile_count = own.shape[2] // LANES
    gx, gy = lax.axis_index("gx"), lax.axis_index("gy")
    up, down = lax.rem(gx + n_rows - 1, n_rows), lax.rem(gx + 1, n_rows)
    left, right = lax.rem(gy + n_cols - 1, n_cols), lax.rem(gy + 1, n_cols)
    corner_ids = [((up, down)[r], (left, right)[s]) for r, s in CORNERS]

    def row_mate(k):
        return (gx, lax.rem(gy + k, n_cols))

    barrier = pltpu.get_barrier_semaphore()
    friends = [row_mate(k) for k in range(1, n_cols)] + [(up, gy), (down, gy)] + corner_ids
    for friend in friends:
        pl.semaphore_signal(barrier, inc=1, device_id=friend, device_id_type=MESH)

    loads = [
        pltpu.make_async_copy(wet_hbm, wet, load_sem.at[0]),
        pltpu.make_async_copy(migration_hbm, migration, load_sem.at[1]),
        pltpu.make_async_copy(migration_hbm, homes.at[0], load_sem.at[2]),
        pltpu.make_async_copy(depth_hbm, own.at[0], load_sem.at[3]),
        pltpu.make_async_copy(velocity_hbm, own.at[pl.ds(1, 2)], load_sem.at[4]),
        pltpu.make_async_copy(bed_hbm, own.at[3], load_sem.at[5]),
    ]
    for load in loads:
        load.start()
    for load in loads:
        load.wait()

    lane = lanes_of((ROWS, LANES))
    packed = jnp.zeros((ROWS, LANES), jnp.float32)
    for f in range(4):
        first, last = own[f, :, 0:LANES], own[f, :, (tile_count - 1) * LANES : tile_count * LANES]
        at = REACH * f
        packed = jnp.where((lane >= at) & (lane < at + REACH), turn(first, at, 1) if f else first, packed)
        at = LANES - REACH * (f + 1)
        packed = jnp.where((lane >= at) & (lane < at + REACH), turn(last, -REACH * f, 1) if f else last, packed)
    for t in range(tile_count):
        packed = jnp.where(lane == WET_LANE + t, wet[0, t].astype(jnp.float32), packed)
    strip[...] = packed

    pl.semaphore_wait(barrier, len(friends))

    def remote(source, target, send, receive, where):
        return pltpu.make_async_remote_copy(
            src_ref=source, dst_ref=target, send_sem=send, recv_sem=receive, device_id=where, device_id_type=MESH
        )

    halos = [
        remote(own, below, halo_send.at[0], halo_recv.at[0], (up, gy)),
        remote(own, above, halo_send.at[1], halo_recv.at[1], (down, gy)),
    ]
    places = [(up, gy), (down, gy), (gx, left), (gx, right)]
    sides = [
        remote(strip, strips.at[i], strip_send.at[i], strip_recv.at[i], where) for i, where in enumerate(places)
    ]
    diagonals = [
        remote(strip, corners.at[i], corner_send.at[i], corner_recv.at[i], where)
        for i, where in enumerate(corner_ids)
    ]
    mates = [
        remote(homes.at[0], homes.at[k], home_send.at[k], home_recv.at[k], row_mate(k)) for k in range(1, n_cols)
    ]
    for copy in sides + diagonals + halos + mates:
        copy.start()

    chosen = []
    for k in range(n_cols):
        target = row_mate(k)[1]
        index = jnp.int32(0)
        for t in range(1, tile_count):
            index = jnp.where(migration[0, t] == target, t, index)
        chosen.append(index)

    for copy in sides + diagonals + halos:
        copy.wait_recv()

    def columns(reference, f):
        return [reference[f, :, c * LANES : (c + 1) * LANES] for c in range(tile_count)]

    def ends(from_left, from_right, f):
        head = turn(from_right, -REACH * f, 1) if f else from_right
        tail = turn(from_left, REACH * f, 1) if f else from_left
        return jnp.where(lane < REACH, head, jnp.where(lane >= LANES - REACH, tail, 0.0))

    lower_right, upper_right, lower_left, upper_left = (corners[i] for i in range(4))
    bands = (
        (above, upper_left, upper_right, strips[1]),
        (own, strips[3], strips[2], strip[...]),
        (below, lower_left, lower_right, strips[0]),
    )
    fields = []
    for f in range(4):
        stacked = [columns(band[0], f) + [ends(band[1], band[2], f)] for band in bands]
        fields.append([jnp.concatenate([s[c] for s in stacked], axis=0) for c in range(tile_count + 1)])

    def spread(tile, at):
        return jnp.broadcast_to(tile[:, at : at + 1], (ROWS, LANES))

    wets = []
    for c in range(tile_count + 1):
        stacked = []
        for _, from_left, from_right, flags in bands:
            if c < tile_count:
                stacked.append(spread(flags, WET_LANE + c))
            else:
                stacked.append(
                    jnp.where(
                        lane < LANES // 2, spread(from_right, WET_LANE), spread(from_left, WET_LANE + tile_count - 1)
                    )
                )
        wets.append(jnp.concatenate(stacked, axis=0))

    row = lax.broadcasted_iota(jnp.int32, (3 * ROWS, LANES), 0)
    wide = lanes_of((3 * ROWS, LANES))
    one, zero = jnp.float32(1), jnp.float32(0)
    has_up, has_down = jnp.where(gx > 0, one, zero), jnp.where(gx < n_rows - 1, one, zero)
    has_left, has_right = jnp.where(gy > 0, one, zero), jnp.where(gy < n_cols - 1, one, zero)
    inside_rows = jnp.where(row < ROWS, has_up, jnp.where(row >= 2 * ROWS, has_down, one))
    inside_ends = inside_rows * jnp.where(wide < LANES // 2, has_right, has_left)
    masks = [inside_rows] * tile_count + [inside_ends]

    depth, across, along, bed = fields
    state = []
    beds = []
    for c in range(tile_count + 1):
        h = depth[c] * masks[c]
        state.append((h, h * across[c], h * along[c]))
        beds.append(bed[c] * masks[c])
    bed_next, bed_previous = ring_next(beds), ring_previous(beds)
    slopes = [
        (
            (0.5 * COURANT) * (bed_next[c] - bed_previous[c]),
            (0.5 * COURANT) * (turn(beds[c], -1, 0) - turn(beds[c], 1, 0)),
        )
        for c in range(tile_count + 1)
    ]
    advanced = two_steps(state, slopes, masks)
    state = [
        tuple(jnp.where(w > 0.5, new, old) for new, old in zip(a, s)) for w, a, s in zip(wets, advanced, state)
    ]

    def narrow(x, start, size):
        return turn(x, -start, 0)[:size]

    kept = 2 * HALO + ROWS
    state = [tuple(narrow(x, ROWS - HALO, kept) for x in s) for s in state]
    slopes = [tuple(narrow(x, ROWS - HALO, kept) for x in s) for s in slopes]
    masks = [narrow(x, ROWS - HALO, kept) for x in masks]
    advanced = two_steps(state, slopes, masks)
    for t in range(tile_count):
        for f in range(3):
            new, old = narrow(advanced[t][f], HALO, ROWS), narrow(state[t][f], HALO, ROWS)
            tiles[t, f] = jnp.where(wets[t][ROWS : 2 * ROWS] > 0.5, new, old)

    slots = []
    for k in sorted(range(1, n_cols), key=lambda k: -min(k, n_cols - k)):
        outgoing[k] = tiles[chosen[k]]
        copy = remote(outgoing.at[k], arrived.at[k], slot_send.at[k], slot_recv.at[k], row_mate(k))
        copy.start()
        slots.append(copy)
    arrived[0] = tiles[chosen[0]]

    for copy in mates:
        copy.wait_recv()
    flat = pltpu.make_async_copy(homes, homes_flat, flat_sem.at[0])
    flat.start()
    flat.wait()
    sources = []
    for t in range(tile_count):
        index = jnp.int32(0)
        for k in range(1, n_cols):
            index = jnp.where(homes_flat[k, 0, t] == gy, k, index)
        sources.append(index)
    for copy in slots:
        copy.wait_recv()
    for t in range(tile_count):
        out_ref[:, :, t * LANES : (t + 1) * LANES] = arrived[sources[t]]
    for copy in sides + diagonals + halos + mates + slots:
        copy.wait_send()


def solution(mesh):
    n_rows, n_cols = mesh.shape["gx"], mesh.shape["gy"]

    def step(water_depth, velocity, bathymetry, wet_tiles, migration):
        rows, cols = water_depth.shape
        tile_count = wet_tiles.shape[1]
        block = (4, rows, cols)
        dma = pltpu.SemaphoreType.DMA
        return pl.pallas_call(
            functools.partial(kernel, (n_rows, n_cols)),
            out_shape=jax.ShapeDtypeStruct((3, rows, cols), jnp.float32),
            in_specs=[pl.BlockSpec(memory_space=pl.ANY)] * 5,
            out_specs=pl.BlockSpec(memory_space=pltpu.VMEM),
            scratch_shapes=[
                pltpu.VMEM(block, jnp.float32),
                pltpu.VMEM(block, jnp.float32),
                pltpu.VMEM(block, jnp.float32),
                pltpu.VMEM((ROWS, LANES), jnp.float32),
                pltpu.VMEM((4, ROWS, LANES), jnp.float32),
                pltpu.VMEM((4, ROWS, LANES), jnp.float32),
                pltpu.SMEM((1, tile_count), jnp.int32),
                pltpu.SMEM((1, tile_count), jnp.int32),
                pltpu.VMEM((n_cols, 1, tile_count), jnp.int32),
                pltpu.SMEM((n_cols, 1, tile_count), jnp.int32),
                pltpu.VMEM((tile_count, 3, rows, LANES), jnp.float32),
                pltpu.VMEM((n_cols, 3, rows, LANES), jnp.float32),
                pltpu.VMEM((n_cols, 3, rows, LANES), jnp.float32),
                dma((6,)),
                dma((1,)),
                dma((2,)),
                dma((2,)),
                dma((4,)),
                dma((4,)),
                dma((4,)),
                dma((4,)),
                dma((n_cols,)),
                dma((n_cols,)),
                dma((n_cols,)),
                dma((n_cols,)),
            ],
            compiler_params=pltpu.CompilerParams(
                collective_id=0, has_side_effects=True, vmem_limit_bytes=32 * 1024 * 1024
            ),
        )(water_depth, velocity, bathymetry, wet_tiles, migration)

    return jax.shard_map(
        step,
        mesh=mesh,
        in_specs=(P("gx", "gy"), P(None, "gx", "gy"), P("gx", "gy"), P("gx", "gy"), P("gx", "gy")),
        out_specs=P(None, "gx", "gy"),
        check_vma=False,
    )
```

profile of v0, /device:TPU:1, one launch (start us, length us, event | category | flops | bytes accessed | tf_op | source)
XLA Modules:
  0.0 43.3 jit_solution(2634250307722463204)
XLA Ops:
  0.0 0.0 copy-start
  0.0 0.8 %copy-done = f32[2,8,1024]{2,1,0:T(8,128)S(1)} copy-done((f32[2,8,1024]{2,1,0:T(8,128)S(1)}, f32[2,8,1024]{2,1,0:T(8,128)}, u32[]{:S(2)}) %copy-start) | copy-done | bytes 65560
  0.8 0.0 copy-start.1
  0.8 0.8 %copy-done.1 = f32[8,1024]{1,0:T(8,128)S(1)} copy-done((f32[8,1024]{1,0:T(8,128)S(1)}, f32[8,1024]{1,0:T(8,128)}, u32[]{:S(2)}) %copy-start.1) | copy-done | bytes 32792
  1.6 0.0 copy-start.2
  1.6 0.8 %copy-done.2 = f32[8,1024]{1,0:T(8,128)S(1)} copy-done((f32[8,1024]{1,0:T(8,128)S(1)}, f32[8,1024]{1,0:T(8,128)}, u32[]{:S(2)}) %copy-start.2) | copy-done | bytes 32792
  2.4 0.0 copy-start.3
  2.4 0.7 %copy-done.3 = s32[1,8]{1,0:T(1,128)S(1)} copy-done((s32[1,8]{1,0:T(1,128)S(1)}, s32[1,8]{1,0:T(1,128)}, u32[]{:S(2)}) %copy-start.3) | copy-done | bytes 56
  3.0 0.0 copy-start.4
  3.0 0.7 %copy-done.4 = s32[1,8]{1,0:T(1,128)S(1)} copy-done((s32[1,8]{1,0:T(1,128)S(1)}, s32[1,8]{1,0:T(1,128)}, u32[]{:S(2)}) %copy-start.4) | copy-done | bytes 56
  3.7 39.0 %shard_map.55 = f32[3,8,1024]{2,1,0:T(8,128)S(1)} custom-call(f32[8,1024]{1,0:T(8,128)S(1)} %copy-done.1, f32[2,8,1024]{2,1,0:T(8,128)S(1)} %copy-done, f32[8,1024]{1,0:T(8,128)S(1)} %copy-done.2, s32[1,8]{1,0:T(1,128)S(1)} %copy-done.3, s32[1,8]{1,0:T(1,128)S(1)} %copy-done.4), custom_call_target="tpu_custom_call" | custom-call | tf_op jit(solution)/shard_map/pallas_call | solution.py:322
  42.7 0.6 %copy.7 = f32[3,8,1024]{2,1,0:T(8,128)} copy(f32[3,8,1024]{2,1,0:T(8,128)S(1)} %shard_map.55) | data formatting | bytes 196608
Async XLA Ops:
  0.0 0.8 %copy-start = (f32[2,8,1024]{2,1,0:T(8,128)S(1)}, f32[2,8,1024]{2,1,0:T(8,128)}, u32[]{:S(2)}) copy-start(f32[2,8,1024]{2,1,0:T(8,128)} %velocity_hbm.1) | copy-start | bytes 196612
  0.8 0.8 %copy-start.1 = (f32[8,1024]{1,0:T(8,128)S(1)}, f32[8,1024]{1,0:T(8,128)}, u32[]{:S(2)}) copy-start(f32[8,1024]{1,0:T(8,128)} %depth_hbm.1) | copy-start | bytes 98308
  1.6 0.8 %copy-start.2 = (f32[8,1024]{1,0:T(8,128)S(1)}, f32[8,1024]{1,0:T(8,128)}, u32[]{:S(2)}) copy-start(f32[8,1024]{1,0:T(8,128)} %bed_hbm.1) | copy-start | bytes 98308
  2.4 0.7 %copy-start.3 = (s32[1,8]{1,0:T(1,128)S(1)}, s32[1,8]{1,0:T(1,128)}, u32[]{:S(2)}) copy-start(s32[1,8]{1,0:T(1,128)} %wet_hbm.1) | copy-start | bytes 100
  3.0 0.7 %copy-start.4 = (s32[1,8]{1,0:T(1,128)S(1)}, s32[1,8]{1,0:T(1,128)}, u32[]{:S(2)}) copy-start(s32[1,8]{1,0:T(1,128)} %migration_hbm.1) | copy-start | bytes 100
where the time goes:
time: 43.7 us; the launch traced here: 43.3 us
  Pallas kernels  39 us (89%)
  local copies, waits for them, and re-layouts  4.31 us (10%)
    pallas_call x1, Pallas kernels, step(): pl.pallas_call(functools.partial(kernel, (n_rows, n_cols)), out_shape=jax...  39 us
    unnamed x11, local copies, waits for them, and re-layouts  4.31 us

commit v1 on v0

--- a/solution.py
+++ b/solution.py
@@ -111,14 +111,11 @@
     strips,
     corners,
     wet,
-    migration,
     homes,
-    homes_flat,
     tiles,
     outgoing,
     arrived,
     load_sem,
-    flat_sem,
     halo_send,
     halo_recv,
     strip_send,
@@ -133,25 +130,38 @@
     n_rows, n_cols = sizes
     tile_count = own.shape[2] // LANES
     gx, gy = lax.axis_index("gx"), lax.axis_index("gy")
+    has_up, has_down, has_left, has_right = gx > 0, gx < n_rows - 1, gy > 0, gy < n_cols - 1
     up, down = lax.rem(gx + n_rows - 1, n_rows), lax.rem(gx + 1, n_rows)
     left, right = lax.rem(gy + n_cols - 1, n_cols), lax.rem(gy + 1, n_cols)
     corner_ids = [((up, down)[r], (left, right)[s]) for r, s in CORNERS]
+    has_corner = [(has_up, has_down)[r] & (has_left, has_right)[s] for r, s in CORNERS]
 
     def row_mate(k):
         return (gx, lax.rem(gy + k, n_cols))
 
+    def remote(source, target, send, receive, where):
+        return pltpu.make_async_remote_copy(
+            src_ref=source, dst_ref=target, send_sem=send, recv_sem=receive, device_id=where, device_id_type=MESH
+        )
+
     barrier = pltpu.get_barrier_semaphore()
-    friends = [row_mate(k) for k in range(1, n_cols)] + [(up, gy), (down, gy)] + corner_ids
-    for friend in friends:
+
+    def greet(friend):
         pl.semaphore_signal(barrier, inc=1, device_id=friend, device_id_type=MESH)
 
+    beyond = [(has_up, (up, gy)), (has_down, (down, gy))] + list(zip(has_corner, corner_ids))
+    for there, friend in beyond:
+        pl.when(there)(functools.partial(greet, friend))
+    for k in range(1, n_cols):
+        greet(row_mate(k))
+    friends = n_cols - 1 + sum(there.astype(jnp.int32) for there, _ in beyond)
+
     loads = [
-        pltpu.make_async_copy(wet_hbm, wet, load_sem.at[0]),
-        pltpu.make_async_copy(migration_hbm, migration, load_sem.at[1]),
-        pltpu.make_async_copy(migration_hbm, homes.at[0], load_sem.at[2]),
-        pltpu.make_async_copy(depth_hbm, own.at[0], load_sem.at[3]),
-        pltpu.make_async_copy(velocity_hbm, own.at[pl.ds(1, 2)], load_sem.at[4]),
-        pltpu.make_async_copy(bed_hbm, own.at[3], load_sem.at[5]),
+        pltpu.make_async_copy(depth_hbm, own.at[0], load_sem.at[0]),
+        pltpu.make_async_copy(velocity_hbm, own.at[pl.ds(1, 2)], load_sem.at[1]),
+        pltpu.make_async_copy(bed_hbm, own.at[3], load_sem.at[2]),
+        pltpu.make_async_copy(wet_hbm, wet, load_sem.at[3]),
+        pltpu.make_async_copy(migration_hbm, homes.at[0], load_sem.at[4]),
     ]
     for load in loads:
         load.start()
@@ -170,41 +180,40 @@
         packed = jnp.where(lane == WET_LANE + t, wet[0, t].astype(jnp.float32), packed)
     strip[...] = packed
 
-    pl.semaphore_wait(barrier, len(friends))
-
-    def remote(source, target, send, receive, where):
-        return pltpu.make_async_remote_copy(
-            src_ref=source, dst_ref=target, send_sem=send, recv_sem=receive, device_id=where, device_id_type=MESH
-        )
-
-    halos = [
-        remote(own, below, halo_send.at[0], halo_recv.at[0], (up, gy)),
-        remote(own, above, halo_send.at[1], halo_recv.at[1], (down, gy)),
-    ]
-    places = [(up, gy), (down, gy), (gx, left), (gx, right)]
-    sides = [
-        remote(strip, strips.at[i], strip_send.at[i], strip_recv.at[i], where) for i, where in enumerate(places)
-    ]
-    diagonals = [
-        remote(strip, corners.at[i], corner_send.at[i], corner_recv.at[i], where)
-        for i, where in enumerate(corner_ids)
-    ]
+    pl.semaphore_wait(barrier, friends)
+
+    ways = [(has_up, (up, gy), below), (has_down, (down, gy), above), (has_left, (gx, left), None), (has_right, (gx, right), None)]
+    halos = []
+    for i, (there, where, target) in enumerate(ways):
+        copies = [remote(strip, strips.at[i], strip_send.at[i], strip_recv.at[i], where)]
+        if target is not None:
+            copies.append(remote(own, target, halo_send.at[i], halo_recv.at[i], where))
+        halos.append((there, copies))
+    for i, (there, where) in enumerate(zip(has_corner, corner_ids)):
+        halos.append((there, [remote(strip, corners.at[i], corner_send.at[i], corner_recv.at[i], where)]))
+    opposite = [1, 0, 3, 2, 7, 6, 5, 4]
     mates = [
         remote(homes.at[0], homes.at[k], home_send.at[k], home_recv.at[k], row_mate(k)) for k in range(1, n_cols)
     ]
-    for copy in sides + diagonals + halos + mates:
-        copy.start()
+
+    def each(copies, what):
+        for copy in copies:
+            getattr(copy, what)()
+
+    for there, copies in halos:
+        pl.when(there)(functools.partial(each, copies, "start"))
+    each(mates, "start")
 
     chosen = []
     for k in range(n_cols):
         target = row_mate(k)[1]
         index = jnp.int32(0)
         for t in range(1, tile_count):
-            index = jnp.where(migration[0, t] == target, t, index)
+            index = jnp.where(homes[0, 0, t] == target, t, index)
         chosen.append(index)
 
-    for copy in sides + diagonals + halos:
-        copy.wait_recv()
+    for (there, _), i in zip(halos, opposite):
+        pl.when(there)(functools.partial(each, halos[i][1], "wait_recv"))
 
     def columns(reference, f):
         return [reference[f, :, c * LANES : (c + 1) * LANES] for c in range(tile_count)]
@@ -244,20 +253,13 @@
 
     row = lax.broadcasted_iota(jnp.int32, (3 * ROWS, LANES), 0)
     wide = lanes_of((3 * ROWS, LANES))
-    one, zero = jnp.float32(1), jnp.float32(0)
-    has_up, has_down = jnp.where(gx > 0, one, zero), jnp.where(gx < n_rows - 1, one, zero)
-    has_left, has_right = jnp.where(gy > 0, one, zero), jnp.where(gy < n_cols - 1, one, zero)
-    inside_rows = jnp.where(row < ROWS, has_up, jnp.where(row >= 2 * ROWS, has_down, one))
-    inside_ends = inside_rows * jnp.where(wide < LANES // 2, has_right, has_left)
+    weights = [there.astype(jnp.float32) for there in (has_up, has_down, has_left, has_right)]
+    inside_rows = jnp.where(row < ROWS, weights[0], jnp.where(row >= 2 * ROWS, weights[1], jnp.float32(1)))
+    inside_ends = inside_rows * jnp.where(wide < LANES // 2, weights[3], weights[2])
     masks = [inside_rows] * tile_count + [inside_ends]
 
-    depth, across, along, bed = fields
-    state = []
-    beds = []
-    for c in range(tile_count + 1):
-        h = depth[c] * masks[c]
-        state.append((h, h * across[c], h * along[c]))
-        beds.append(bed[c] * masks[c])
+    depth, across, along, beds = ([jnp.where(m > 0.5, x, 0.0) for m, x in zip(masks, field)] for field in fields)
+    state = [(depth[c], depth[c] * across[c], depth[c] * along[c]) for c in range(tile_count + 1)]
     bed_next, bed_previous = ring_next(beds), ring_previous(beds)
     slopes = [
         (
@@ -292,23 +294,19 @@
         slots.append(copy)
     arrived[0] = tiles[chosen[0]]
 
-    for copy in mates:
-        copy.wait_recv()
-    flat = pltpu.make_async_copy(homes, homes_flat, flat_sem.at[0])
-    flat.start()
-    flat.wait()
+    each(mates, "wait_recv")
     sources = []
     for t in range(tile_count):
         index = jnp.int32(0)
         for k in range(1, n_cols):
-            index = jnp.where(homes_flat[k, 0, t] == gy, k, index)
+            index = jnp.where(homes[k, 0, t] == gy, k, index)
         sources.append(index)
-    for copy in slots:
-        copy.wait_recv()
+    each(slots, "wait_recv")
     for t in range(tile_count):
         out_ref[:, :, t * LANES : (t + 1) * LANES] = arrived[sources[t]]
-    for copy in sides + diagonals + halos + mates + slots:
-        copy.wait_send()
+    for there, copies in halos:
+        pl.when(there)(functools.partial(each, copies, "wait_send"))
+    each(mates + slots, "wait_send")
 
 
 def solution(mesh):
@@ -332,14 +330,11 @@
                 pltpu.VMEM((4, ROWS, LANES), jnp.float32),
                 pltpu.VMEM((4, ROWS, LANES), jnp.float32),
                 pltpu.SMEM((1, tile_count), jnp.int32),
-                pltpu.SMEM((1, tile_count), jnp.int32),
-                pltpu.VMEM((n_cols, 1, tile_count), jnp.int32),
                 pltpu.SMEM((n_cols, 1, tile_count), jnp.int32),
                 pltpu.VMEM((tile_count, 3, rows, LANES), jnp.float32),
                 pltpu.VMEM((n_cols, 3, rows, LANES), jnp.float32),
                 pltpu.VMEM((n_cols, 3, rows, LANES), jnp.float32),
-                dma((6,)),
-                dma((1,)),
+                dma((5,)),
                 dma((2,)),
                 dma((2,)),
                 dma((4,)),
@@ -352,7 +347,7 @@
                 dma((n_cols,)),
             ],
             compiler_params=pltpu.CompilerParams(
-                collective_id=0, has_side_effects=True, vmem_limit_bytes=32 * 1024 * 1024
+                collective_id=0, has_side_effects=True, vmem_limit_bytes=60 * 1024 * 1024
             ),
         )(water_depth, velocity, bathymetry, wet_tiles, migration)
 

time: 43.7 us -> 37.9 us (0.87)
  the two profiles are of different devices: /device:TPU:1 before, /device:TPU:97 now
where the time goes in v1:
time: 37.9 us; the launch traced here: 37.7 us
  Pallas kernels  36.2 us (96%)
  local copies, waits for them, and re-layouts  1.54 us (4%)
    pallas_call x1, Pallas kernels, step(): pl.pallas_call(functools.partial(kernel, (n_rows, n_cols)), out_shape=jax...  36.2 us
    unnamed x1, local copies, waits for them, and re-layouts  1.54 us

profile of v1, /device:TPU:97, one launch (start us, length us, event | category | flops | bytes accessed | tf_op | source)
XLA Modules:
  0.0 37.7 jit_solution(12075077378362593409)
XLA Ops:
  0.0 36.2 %shard_map.55 = f32[3,8,1024]{2,1,0:T(8,128)} custom-call(f32[8,1024]{1,0:T(8,128)} %depth_hbm.1, f32[2,8,1024]{2,1,0:T(8,128)} %velocity_hbm.1, f32[8,1024]{1,0:T(8,128)} %bed_hbm.1, s32[1,8]{1,0:T(1,128)} %wet_hbm.1, s32[1,8]{1,0:T(1,128)} %migration_hbm.1), custom_call_target="tpu_custom_call" | custom-call | tf_op jit(solution)/shard_map/pallas_call | solution.py:320
  36.2 1.5 %copy.7 = f32[3,8,1024]{2,1,0:T(8,128)} copy(f32[3,8,1024]{2,1,0:T(8,128)} %shard_map.55) | data formatting | bytes 196608

commit v2 on v1

--- a/solution.py
+++ b/solution.py
@@ -126,6 +126,8 @@
     home_recv,
     slot_send,
     slot_recv,
+    lower,
+    higher,
 ):
     n_rows, n_cols = sizes
     tile_count = own.shape[2] // LANES
@@ -136,9 +138,6 @@
     corner_ids = [((up, down)[r], (left, right)[s]) for r, s in CORNERS]
     has_corner = [(has_up, has_down)[r] & (has_left, has_right)[s] for r, s in CORNERS]
 
-    def row_mate(k):
-        return (gx, lax.rem(gy + k, n_cols))
-
     def remote(source, target, send, receive, where):
         return pltpu.make_async_remote_copy(
             src_ref=source, dst_ref=target, send_sem=send, recv_sem=receive, device_id=where, device_id_type=MESH
@@ -149,19 +148,18 @@
     def greet(friend):
         pl.semaphore_signal(barrier, inc=1, device_id=friend, device_id_type=MESH)
 
-    beyond = [(has_up, (up, gy)), (has_down, (down, gy))] + list(zip(has_corner, corner_ids))
+    beyond = [(has_up, (up, gy)), (has_down, (down, gy)), (has_left, (gx, left)), (has_right, (gx, right))]
+    beyond += list(zip(has_corner, corner_ids))
     for there, friend in beyond:
         pl.when(there)(functools.partial(greet, friend))
-    for k in range(1, n_cols):
-        greet(row_mate(k))
-    friends = n_cols - 1 + sum(there.astype(jnp.int32) for there, _ in beyond)
+    friends = sum(there.astype(jnp.int32) for there, _ in beyond)
 
     loads = [
         pltpu.make_async_copy(depth_hbm, own.at[0], load_sem.at[0]),
         pltpu.make_async_copy(velocity_hbm, own.at[pl.ds(1, 2)], load_sem.at[1]),
         pltpu.make_async_copy(bed_hbm, own.at[3], load_sem.at[2]),
         pltpu.make_async_copy(wet_hbm, wet, load_sem.at[3]),
-        pltpu.make_async_copy(migration_hbm, homes.at[0], load_sem.at[4]),
+        pltpu.make_async_copy(migration_hbm, homes.at[gy], load_sem.at[4]),
     ]
     for load in loads:
         load.start()
@@ -192,24 +190,36 @@
     for i, (there, where) in enumerate(zip(has_corner, corner_ids)):
         halos.append((there, [remote(strip, corners.at[i], corner_send.at[i], corner_recv.at[i], where)]))
     opposite = [1, 0, 3, 2, 7, 6, 5, 4]
-    mates = [
-        remote(homes.at[0], homes.at[k], home_send.at[k], home_recv.at[k], row_mate(k)) for k in range(1, n_cols)
-    ]
-
     def each(copies, what):
         for copy in copies:
             getattr(copy, what)()
 
     for there, copies in halos:
         pl.when(there)(functools.partial(each, copies, "start"))
-    each(mates, "start")
+
+    def send_home(target):
+        remote(homes.at[gy], homes.at[gy], home_send, home_recv, (gx, target)).start()
+
+    def announce(target, carry):
+        pl.semaphore_signal(higher, inc=1, device_id=(gx, target), device_id_type=MESH)
+        send_home(target)
+        return carry
+
+    @pl.when(has_left)
+    def _():
+        pl.semaphore_wait(lower, 1)
+
+    @pl.when(has_right)
+    def _():
+        pl.semaphore_signal(lower, inc=1, device_id=(gx, right), device_id_type=MESH)
+
+    lax.fori_loop(0, gy, announce, 0)
 
     chosen = []
-    for k in range(n_cols):
-        target = row_mate(k)[1]
+    for target in range(n_cols):
         index = jnp.int32(0)
         for t in range(1, tile_count):
-            index = jnp.where(homes[0, 0, t] == target, t, index)
+            index = jnp.where(homes[gy, 0, t] == target, t, index)
         chosen.append(index)
 
     for (there, _), i in zip(halos, opposite):
@@ -286,27 +296,47 @@
             new, old = narrow(advanced[t][f], HALO, ROWS), narrow(state[t][f], HALO, ROWS)
             tiles[t, f] = jnp.where(wets[t][ROWS : 2 * ROWS] > 0.5, new, old)
 
-    slots = []
-    for k in sorted(range(1, n_cols), key=lambda k: -min(k, n_cols - k)):
-        outgoing[k] = tiles[chosen[k]]
-        copy = remote(outgoing.at[k], arrived.at[k], slot_send.at[k], slot_recv.at[k], row_mate(k))
-        copy.start()
-        slots.append(copy)
-    arrived[0] = tiles[chosen[0]]
-
-    each(mates, "wait_recv")
+    for target in range(n_cols):
+        outgoing[target] = tiles[chosen[target]]
+    arrived[gy] = outgoing[gy]
+
+    def send_slot(target):
+        remote(outgoing.at[target], arrived.at[gy], slot_send, slot_recv, (gx, target)).start()
+
+    def to_lower(target, carry):
+        send_slot(target)
+        return carry
+
+    def to_higher(target, carry):
+        send_home(target)
+        send_slot(target)
+        return carry
+
+    lax.fori_loop(0, gy, to_lower, 0)
+
+    @pl.when(has_right)
+    def _():
+        pl.semaphore_wait(higher, n_cols - 1 - gy)
+
+    lax.fori_loop(gy + 1, n_cols, to_higher, 0)
+
+    others = pl.ds(0, n_cols - 1)
+    all_homes = remote(homes.at[others], homes.at[others], home_send, home_recv, (gx, right))
+    all_slots = remote(outgoing.at[others], arrived.at[others], slot_send, slot_recv, (gx, right))
+    all_homes.wait_recv()
     sources = []
     for t in range(tile_count):
         index = jnp.int32(0)
-        for k in range(1, n_cols):
-            index = jnp.where(homes[k, 0, t] == gy, k, index)
+        for source in range(1, n_cols):
+            index = jnp.where(homes[source, 0, t] == gy, source, index)
         sources.append(index)
-    each(slots, "wait_recv")
+    all_slots.wait_recv()
     for t in range(tile_count):
         out_ref[:, :, t * LANES : (t + 1) * LANES] = arrived[sources[t]]
     for there, copies in halos:
         pl.when(there)(functools.partial(each, copies, "wait_send"))
-    each(mates + slots, "wait_send")
+    all_homes.wait_send()
+    all_slots.wait_send()
 
 
 def solution(mesh):
@@ -319,7 +349,7 @@
         dma = pltpu.SemaphoreType.DMA
         return pl.pallas_call(
             functools.partial(kernel, (n_rows, n_cols)),
-            out_shape=jax.ShapeDtypeStruct((3, rows, cols), jnp.float32),
+            out_shape=pltpu.VMEM((3, rows, cols), jnp.float32),
             in_specs=[pl.BlockSpec(memory_space=pl.ANY)] * 5,
             out_specs=pl.BlockSpec(memory_space=pltpu.VMEM),
             scratch_shapes=[
@@ -341,15 +371,17 @@
                 dma((4,)),
                 dma((4,)),
                 dma((4,)),
-                dma((n_cols,)),
-                dma((n_cols,)),
-                dma((n_cols,)),
-                dma((n_cols,)),
+                dma,
+                dma,
+                dma,
+                dma,
+                pltpu.SemaphoreType.REGULAR,
+                pltpu.SemaphoreType.REGULAR,
             ],
             compiler_params=pltpu.CompilerParams(
-                collective_id=0, has_side_effects=True, vmem_limit_bytes=60 * 1024 * 1024
+                collective_id=0, has_side_effects=True, vmem_limit_bytes=32 * 1024 * 1024
             ),
-        )(water_depth, velocity, bathymetry, wet_tiles, migration)
+        )(*(pltpu.with_memory_space_constraint(x, pltpu.HBM) for x in (water_depth, velocity, bathymetry, wet_tiles, migration)))
 
     return jax.shard_map(
         step,

time: 37.9 us -> 33.2 us (0.88)
  the two profiles are of different devices: /device:TPU:97 before, /device:TPU:65 now
where the time goes in v2:
time: 33.2 us; the launch traced here: 33 us
  Pallas kernels  32.4 us (98%)
  local copies, waits for them, and re-layouts  0.64 us (2%)
    pallas_call x1, Pallas kernels, step(): pl.pallas_call(functools.partial(kernel, (n_rows, n_cols)), out_shape=plt...  32.4 us

profile of v2, /device:TPU:65, one launch (start us, length us, event | category | flops | bytes accessed | tf_op | source)
XLA Modules:
  0.0 33.0 jit_solution(12164788912925511464)
XLA Ops:
  0.0 32.4 %shard_map.55 = f32[3,8,1024]{2,1,0:T(8,128)S(1)} custom-call(f32[8,1024]{1,0:T(8,128)} %depth_hbm.1, f32[2,8,1024]{2,1,0:T(8,128)} %velocity_hbm.1, f32[8,1024]{1,0:T(8,128)} %bed_hbm.1, s32[1,8]{1,0:T(1,128)} %wet_hbm.1, s32[1,8]{1,0:T(1,128)} %migration_hbm.1), custom_call_target="tpu_custom_call" | custom-call | tf_op jit(solution)/shard_map/pallas_call | solution.py:350
  32.4 0.6 %copy.7 = f32[3,8,1024]{2,1,0:T(8,128)} copy(f32[3,8,1024]{2,1,0:T(8,128)S(1)} %shard_map.55) | data formatting | bytes 196608

commit v3 on v2

--- a/solution.py
+++ b/solution.py
@@ -12,6 +12,7 @@
 HALO = 4
 ROWS = 8
 LANES = 128
+TAG = 3 * ROWS
 REACH = 8
 WET_LANE = 32
 MESH = pl.DeviceIdType.MESH
@@ -111,7 +112,7 @@
     strips,
     corners,
     wet,
-    homes,
+    migration,
     tiles,
     outgoing,
     arrived,
@@ -122,8 +123,6 @@
     strip_recv,
     corner_send,
     corner_recv,
-    home_send,
-    home_recv,
     slot_send,
     slot_recv,
     lower,
@@ -150,6 +149,9 @@
 
     beyond = [(has_up, (up, gy)), (has_down, (down, gy)), (has_left, (gx, left)), (has_right, (gx, right))]
     beyond += list(zip(has_corner, corner_ids))
+    second = lax.rem(gy, 2) == 1
+    beyond += [(second & (gy >= 2), (gx, lax.rem(gy + n_cols - 2, n_cols)))]
+    beyond += [(second & (gy + 2 < n_cols), (gx, lax.rem(gy + 2, n_cols)))]
     for there, friend in beyond:
         pl.when(there)(functools.partial(greet, friend))
     friends = sum(there.astype(jnp.int32) for there, _ in beyond)
@@ -159,7 +161,7 @@
         pltpu.make_async_copy(velocity_hbm, own.at[pl.ds(1, 2)], load_sem.at[1]),
         pltpu.make_async_copy(bed_hbm, own.at[3], load_sem.at[2]),
         pltpu.make_async_copy(wet_hbm, wet, load_sem.at[3]),
-        pltpu.make_async_copy(migration_hbm, homes.at[gy], load_sem.at[4]),
+        pltpu.make_async_copy(migration_hbm, migration, load_sem.at[4]),
     ]
     for load in loads:
         load.start()
@@ -197,29 +199,27 @@
     for there, copies in halos:
         pl.when(there)(functools.partial(each, copies, "start"))
 
-    def send_home(target):
-        remote(homes.at[gy], homes.at[gy], home_send, home_recv, (gx, target)).start()
+    @pl.when(gy >= 2)
+    def _():
+        pl.semaphore_wait(lower, 1)
+
+    def pass_on(target):
+        pl.semaphore_signal(lower, inc=1, device_id=(gx, target), device_id_type=MESH)
+
+    pl.when(second & has_right)(functools.partial(pass_on, right))
+    pl.when(second & (gy + 2 < n_cols))(functools.partial(pass_on, lax.rem(gy + 2, n_cols)))
 
     def announce(target, carry):
         pl.semaphore_signal(higher, inc=1, device_id=(gx, target), device_id_type=MESH)
-        send_home(target)
         return carry
-
-    @pl.when(has_left)
-    def _():
-        pl.semaphore_wait(lower, 1)
-
-    @pl.when(has_right)
-    def _():
-        pl.semaphore_signal(lower, inc=1, device_id=(gx, right), device_id_type=MESH)
 
     lax.fori_loop(0, gy, announce, 0)
 
     chosen = []
     for target in range(n_cols):
-        index = jnp.int32(0)
-        for t in range(1, tile_count):
-            index = jnp.where(homes[gy, 0, t] == target, t, index)
+        index = jnp.int32(-1)
+        for t in range(tile_count):
+            index = jnp.where(migration[0, t] == target, t, index)
         chosen.append(index)
 
     for (there, _), i in zip(halos, opposite):
@@ -294,48 +294,42 @@
     for t in range(tile_count):
         for f in range(3):
             new, old = narrow(advanced[t][f], HALO, ROWS), narrow(state[t][f], HALO, ROWS)
-            tiles[t, f] = jnp.where(wets[t][ROWS : 2 * ROWS] > 0.5, new, old)
+            tiles[t, f * ROWS : (f + 1) * ROWS] = jnp.where(wets[t][ROWS : 2 * ROWS] > 0.5, new, old)
 
     for target in range(n_cols):
-        outgoing[target] = tiles[chosen[target]]
+        outgoing[target, : 3 * ROWS] = tiles[jnp.maximum(chosen[target], 0)]
+        outgoing[target, TAG : TAG + 1] = jnp.full((1, LANES), chosen[target].astype(jnp.float32))
     arrived[gy] = outgoing[gy]
 
-    def send_slot(target):
-        remote(outgoing.at[target], arrived.at[gy], slot_send, slot_recv, (gx, target)).start()
-
-    def to_lower(target, carry):
-        send_slot(target)
+    slot = pl.ds(0, TAG + 1)
+
+    def send_slot(target, carry):
+        remote(outgoing.at[target, slot], arrived.at[gy, slot], slot_send, slot_recv, (gx, target)).start()
         return carry
 
-    def to_higher(target, carry):
-        send_home(target)
-        send_slot(target)
-        return carry
-
-    lax.fori_loop(0, gy, to_lower, 0)
+    lax.fori_loop(0, gy, send_slot, 0)
 
     @pl.when(has_right)
     def _():
         pl.semaphore_wait(higher, n_cols - 1 - gy)
 
-    lax.fori_loop(gy + 1, n_cols, to_higher, 0)
+    lax.fori_loop(gy + 1, n_cols, send_slot, 0)
 
     others = pl.ds(0, n_cols - 1)
-    all_homes = remote(homes.at[others], homes.at[others], home_send, home_recv, (gx, right))
-    all_slots = remote(outgoing.at[others], arrived.at[others], slot_send, slot_recv, (gx, right))
-    all_homes.wait_recv()
-    sources = []
+    all_slots = remote(outgoing.at[others, slot], arrived.at[others, slot], slot_send, slot_recv, (gx, right))
+    all_slots.wait_recv()
+    placed = [[jnp.zeros((ROWS, LANES), jnp.float32) for _ in range(3)] for _ in range(tile_count)]
+    for source in range(n_cols):
+        tag = jnp.broadcast_to(arrived[source, TAG : TAG + 1], (ROWS, LANES))
+        cells = [arrived[source, f * ROWS : (f + 1) * ROWS] for f in range(3)]
+        for t in range(tile_count):
+            here = tag == jnp.float32(t)
+            placed[t] = [jnp.where(here, new, old) for new, old in zip(cells, placed[t])]
     for t in range(tile_count):
-        index = jnp.int32(0)
-        for source in range(1, n_cols):
-            index = jnp.where(homes[source, 0, t] == gy, source, index)
-        sources.append(index)
-    all_slots.wait_recv()
-    for t in range(tile_count):
-        out_ref[:, :, t * LANES : (t + 1) * LANES] = arrived[sources[t]]
+        for f in range(3):
+            out_ref[f, :, t * LANES : (t + 1) * LANES] = placed[t][f]
     for there, copies in halos:
         pl.when(there)(functools.partial(each, copies, "wait_send"))
-    all_homes.wait_send()
     all_slots.wait_send()
 
 
@@ -360,10 +354,10 @@
                 pltpu.VMEM((4, ROWS, LANES), jnp.float32),
                 pltpu.VMEM((4, ROWS, LANES), jnp.float32),
                 pltpu.SMEM((1, tile_count), jnp.int32),
-                pltpu.SMEM((n_cols, 1, tile_count), jnp.int32),
-                pltpu.VMEM((tile_count, 3, rows, LANES), jnp.float32),
-                pltpu.VMEM((n_cols, 3, rows, LANES), jnp.float32),
-                pltpu.VMEM((n_cols, 3, rows, LANES), jnp.float32),
+                pltpu.SMEM((1, tile_count), jnp.int32),
+                pltpu.VMEM((tile_count, 3 * rows, LANES), jnp.float32),
+                pltpu.VMEM((n_cols, 4 * rows, LANES), jnp.float32),
+                pltpu.VMEM((n_cols, 4 * rows, LANES), jnp.float32),
                 dma((5,)),
                 dma((2,)),
                 dma((2,)),
@@ -373,8 +367,6 @@
                 dma((4,)),
                 dma,
                 dma,
-                dma,
-                dma,
                 pltpu.SemaphoreType.REGULAR,
                 pltpu.SemaphoreType.REGULAR,
             ],

time: 33.2 us -> 33.3 us (level)
  the two profiles are of different devices: /device:TPU:65 before, /device:TPU:63 now
where the time goes in v3:
time: 33.3 us; the launch traced here: 33.1 us
  Pallas kernels  32.5 us (98%)
  local copies, waits for them, and re-layouts  0.64 us (2%)
    pallas_call x1, Pallas kernels, step(): pl.pallas_call(functools.partial(kernel, (n_rows, n_cols)), out_shape=plt...  32.5 us

profile of v3, /device:TPU:63, one launch (start us, length us, event | category | flops | bytes accessed | tf_op | source)
XLA Modules:
  0.0 33.1 jit_solution(15620323985341929148)
XLA Ops:
  0.0 32.5 %shard_map.55 = f32[3,8,1024]{2,1,0:T(8,128)S(1)} custom-call(f32[8,1024]{1,0:T(8,128)} %depth_hbm.1, f32[2,8,1024]{2,1,0:T(8,128)} %velocity_hbm.1, f32[8,1024]{1,0:T(8,128)} %bed_hbm.1, s32[1,8]{1,0:T(1,128)} %wet_hbm.1, s32[1,8]{1,0:T(1,128)} %migration_hbm.1), custom_call_target="tpu_custom_call" | custom-call | tf_op jit(solution)/shard_map/pallas_call | solution.py:344
  32.5 0.6 %copy.7 = f32[3,8,1024]{2,1,0:T(8,128)} copy(f32[3,8,1024]{2,1,0:T(8,128)S(1)} %shard_map.55) | data formatting | bytes 196608

commit v4 on v3

--- a/solution.py
+++ b/solution.py
@@ -13,6 +13,7 @@
 ROWS = 8
 LANES = 128
 TAG = 3 * ROWS
+GROUP, GROUP_2 = 2, 2
 REACH = 8
 WET_LANE = 32
 MESH = pl.DeviceIdType.MESH
@@ -27,67 +28,85 @@
     return pltpu.roll(x, by % x.shape[axis], axis)
 
 
-def ring_next(tiles):
-    turned = [turn(x, -1, 1) for x in tiles]
-    last = lanes_of(turned[0].shape) == LANES - 1
-    return [jnp.where(last, turned[(c + 1) % len(tiles)], turned[c]) for c in range(len(tiles))]
-
-
-def ring_previous(tiles):
-    turned = [turn(x, 1, 1) for x in tiles]
-    first = lanes_of(turned[0].shape) == 0
-    return [jnp.where(first, turned[c - 1], turned[c]) for c in range(len(tiles))]
-
-
-def rates(state):
-    parts = []
-    for h, p, q in state:
-        floored = jnp.maximum(h, DRY_DEPTH)
-        inverse_root = lax.rsqrt(floored)
-        celerity = floored * inverse_root
-        inverse = inverse_root * inverse_root
-        u = p * inverse
-        v = q * inverse
-        pressure = 0.5 * h * h
-        parts.append(
-            (h, p, q, p * u + pressure, q * u, q * v + pressure, jnp.abs(u) + celerity, jnp.abs(v) + celerity)
-        )
-    fields = list(zip(*parts))
-    h, p, q, east, cross, north, reach_x, reach_y = fields
-    on = [ring_next(x) for x in (h, p, q, east, cross, reach_x)]
-    faces = [[], [], []]
-    for c in range(len(state)):
-        wave = jnp.maximum(reach_x[c], on[5][c])
-        faces[0].append(p[c] + on[1][c] - wave * (on[0][c] - h[c]))
-        faces[1].append(east[c] + on[3][c] - wave * (on[1][c] - p[c]))
-        faces[2].append(cross[c] + on[4][c] - wave * (on[2][c] - q[c]))
-    back = [ring_previous(x) for x in faces]
-    out = []
-    for c in range(len(state)):
-        below = [turn(x[c], -1, 0) for x in (h, p, q, cross, north, reach_y)]
-        wave = jnp.maximum(reach_y[c], below[5])
-        rows = (
-            q[c] + below[2] - wave * (below[0] - h[c]),
-            cross[c] + below[3] - wave * (below[1] - p[c]),
-            north[c] + below[4] - wave * (below[2] - q[c]),
-        )
-        out.append(
-            tuple((faces[f][c] - back[f][c]) + (rows[f] - turn(rows[f], 1, 0)) for f in range(3))
-        )
-    return out
+def ring_next(x):
+    turned = turn(x, -1, 2)
+    after = jnp.concatenate([turned[1:], turned[:1]], axis=0)
+    return jnp.where(lanes_of(x.shape) == LANES - 1, after, turned)
+
+
+def ring_previous(x):
+    turned = turn(x, 1, 2)
+    before = jnp.concatenate([turned[-1:], turned[:-1]], axis=0)
+    return jnp.where(lanes_of(x.shape) == 0, before, turned)
+
+
+def by_group(function, group, arrays):
+    count = arrays[0].shape[0]
+    pieces = [function(*(x[at : at + group] for x in arrays)) for at in range(0, count, group)]
+    return [jnp.concatenate(column, axis=0) for column in zip(*pieces)]
+
+
+def fluxes(h, p, q):
+    floored = jnp.maximum(h, DRY_DEPTH)
+    inverse_root = lax.rsqrt(floored)
+    celerity = floored * inverse_root
+    inverse = inverse_root * inverse_root
+    u = p * inverse
+    v = q * inverse
+    pressure = 0.5 * h * h
+    east, cross, north = p * u + pressure, q * u, q * v + pressure
+    speed = jnp.abs(u) + celerity
+    turned = tuple(turn(x, -1, 2) for x in (h, p, q, east, cross, speed))
+    return (east, cross, speed, north, jnp.abs(v) + celerity) + turned
+
+
+def faces(h, p, q, flux_h, flux_p, flux_q, speed, h_on, p_on, q_on, flux_h_on, flux_p_on, flux_q_on, speed_on):
+    wave = jnp.maximum(speed, speed_on)
+    return (
+        flux_h + flux_h_on - wave * (h_on - h),
+        flux_p + flux_p_on - wave * (p_on - p),
+        flux_q + flux_q_on - wave * (q_on - q),
+    )
+
+
+def column_faces(h, p, q, east, cross, speed, *turned):
+    count = h.shape[0]
+    last = lanes_of(h.shape) == LANES - 1
+    h_on, p_on, q_on, east_on, cross_on, speed_on = (
+        jnp.where(last, after, x) for x, after in zip(turned[:6], turned[6:])
+    )
+    values = faces(h, p, q, p, east, cross, speed, h_on, p_on, q_on, p_on, east_on, cross_on, speed_on)
+    return values + tuple(turn(x, 1, 2) for x in values)
+
+
+def update(h, p, q, cross, north, speed, *rest):
+    columns, slopes, mask, start = rest[:9], rest[9:11], rest[11], rest[12:]
+    hb, pb, qb, cross_b, north_b, speed_b = (turn(x, -1, 1) for x in (h, p, q, cross, north, speed))
+    rows = faces(h, p, q, q, cross, north, speed, hb, pb, qb, qb, cross_b, north_b, speed_b)
+    first = lanes_of(h.shape) == 0
+    moved = []
+    for f, cells in enumerate((h, p, q)):
+        face, back, before = columns[f::3]
+        change = (face - jnp.where(first, before, back)) + (rows[f] - turn(rows[f], 1, 1))
+        new = cells - (0.5 * COURANT) * change
+        if f:
+            new = new - h * slopes[f - 1]
+        if start:
+            new = 0.5 * start[f] + 0.5 * new
+        moved.append(new * mask)
+    return moved
 
 
 def half_step(state, slopes, masks, start):
-    out = []
-    changes = rates(state)
-    for c, (cells, change, slope, mask) in enumerate(zip(state, changes, slopes, masks)):
-        moved = [cells[0] - (0.5 * COURANT) * change[0]]
-        for f in (1, 2):
-            moved.append(cells[f] - (0.5 * COURANT) * change[f] - cells[0] * slope[f - 1])
-        if start is not None:
-            moved = [0.5 * start[c][f] + 0.5 * moved[f] for f in range(3)]
-        out.append(tuple(x * mask for x in moved))
-    return out
+    h, p, q = state
+    group = GROUP if h.shape[1] > 2 * ROWS else GROUP_2
+    east, cross, reach_x, north, reach_y, *turned = by_group(fluxes, group, state)
+    here = [h, p, q, east, cross, reach_x]
+    after = [jnp.concatenate([x[1:], x[:1]], axis=0) for x in turned]
+    columns = by_group(column_faces, group, here + turned + after)
+    before = [jnp.concatenate([x[-1:], x[:-1]], axis=0) for x in columns[3:]]
+    others = columns + before + list(slopes) + [masks] + list(start or ())
+    return by_group(update, group, [h, p, q, cross, north, reach_y] + others)
 
 
 def two_steps(state, slopes, masks):
@@ -149,9 +168,7 @@
 
     beyond = [(has_up, (up, gy)), (has_down, (down, gy)), (has_left, (gx, left)), (has_right, (gx, right))]
     beyond += list(zip(has_corner, corner_ids))
-    second = lax.rem(gy, 2) == 1
-    beyond += [(second & (gy >= 2), (gx, lax.rem(gy + n_cols - 2, n_cols)))]
-    beyond += [(second & (gy + 2 < n_cols), (gx, lax.rem(gy + 2, n_cols)))]
+
     for there, friend in beyond:
         pl.when(there)(functools.partial(greet, friend))
     friends = sum(there.astype(jnp.int32) for there, _ in beyond)
@@ -165,7 +182,25 @@
     ]
     for load in loads:
         load.start()
-    for load in loads:
+    for load in loads[:3]:
+        load.wait()
+
+    pl.semaphore_wait(barrier, friends)
+
+    def each(copies, what):
+        for copy in copies:
+            getattr(copy, what)()
+
+    ways = [(has_up, (up, gy), below), (has_down, (down, gy), above), (has_left, (gx, left), None), (has_right, (gx, right), None)]
+    halos = []
+    for i, (there, where, target) in enumerate(ways):
+        copies = []
+        if target is not None:
+            copies.append(remote(own, target, halo_send.at[i], halo_recv.at[i], where))
+            pl.when(there)(functools.partial(each, copies, "start"))
+        halos.append((there, copies))
+
+    for load in loads[3:]:
         load.wait()
 
     lane = lanes_of((ROWS, LANES))
@@ -180,34 +215,22 @@
         packed = jnp.where(lane == WET_LANE + t, wet[0, t].astype(jnp.float32), packed)
     strip[...] = packed
 
-    pl.semaphore_wait(barrier, friends)
-
-    ways = [(has_up, (up, gy), below), (has_down, (down, gy), above), (has_left, (gx, left), None), (has_right, (gx, right), None)]
-    halos = []
-    for i, (there, where, target) in enumerate(ways):
-        copies = [remote(strip, strips.at[i], strip_send.at[i], strip_recv.at[i], where)]
-        if target is not None:
-            copies.append(remote(own, target, halo_send.at[i], halo_recv.at[i], where))
-        halos.append((there, copies))
+    for i, (there, where, _) in enumerate(ways):
+        copy = remote(strip, strips.at[i], strip_send.at[i], strip_recv.at[i], where)
+        pl.when(there)(copy.start)
+        halos[i][1].append(copy)
     for i, (there, where) in enumerate(zip(has_corner, corner_ids)):
-        halos.append((there, [remote(strip, corners.at[i], corner_send.at[i], corner_recv.at[i], where)]))
+        copy = remote(strip, corners.at[i], corner_send.at[i], corner_recv.at[i], where)
+        pl.when(there)(copy.start)
+        halos.append((there, [copy]))
     opposite = [1, 0, 3, 2, 7, 6, 5, 4]
-    def each(copies, what):
-        for copy in copies:
-            getattr(copy, what)()
-
-    for there, copies in halos:
-        pl.when(there)(functools.partial(each, copies, "start"))
-
-    @pl.when(gy >= 2)
+    @pl.when(has_left)
     def _():
         pl.semaphore_wait(lower, 1)
 
-    def pass_on(target):
-        pl.semaphore_signal(lower, inc=1, device_id=(gx, target), device_id_type=MESH)
-
-    pl.when(second & has_right)(functools.partial(pass_on, right))
-    pl.when(second & (gy + 2 < n_cols))(functools.partial(pass_on, lax.rem(gy + 2, n_cols)))
+    @pl.when(has_right)
+    def _():
+        pl.semaphore_signal(lower, inc=1, device_id=(gx, right), device_id_type=MESH)
 
     def announce(target, carry):
         pl.semaphore_signal(higher, inc=1, device_id=(gx, target), device_id_type=MESH)
@@ -268,33 +291,28 @@
     inside_ends = inside_rows * jnp.where(wide < LANES // 2, weights[3], weights[2])
     masks = [inside_rows] * tile_count + [inside_ends]
 
-    depth, across, along, beds = ([jnp.where(m > 0.5, x, 0.0) for m, x in zip(masks, field)] for field in fields)
-    state = [(depth[c], depth[c] * across[c], depth[c] * along[c]) for c in range(tile_count + 1)]
-    bed_next, bed_previous = ring_next(beds), ring_previous(beds)
-    slopes = [
-        (
-            (0.5 * COURANT) * (bed_next[c] - bed_previous[c]),
-            (0.5 * COURANT) * (turn(beds[c], -1, 0) - turn(beds[c], 1, 0)),
-        )
-        for c in range(tile_count + 1)
-    ]
+    masks = jnp.stack(masks)
+    depth, across, along, beds = (jnp.where(masks > 0.5, jnp.stack(field), 0.0) for field in fields)
+    state = (depth, depth * across, depth * along)
+    slopes = (
+        (0.5 * COURANT) * (ring_next(beds) - ring_previous(beds)),
+        (0.5 * COURANT) * (turn(beds, -1, 1) - turn(beds, 1, 1)),
+    )
+    wets = jnp.stack(wets)
     advanced = two_steps(state, slopes, masks)
-    state = [
-        tuple(jnp.where(w > 0.5, new, old) for new, old in zip(a, s)) for w, a, s in zip(wets, advanced, state)
-    ]
+    state = tuple(jnp.where(wets > 0.5, new, old) for new, old in zip(advanced, state))
 
     def narrow(x, start, size):
-        return turn(x, -start, 0)[:size]
+        return turn(x, -start, 1)[:, :size]
 
     kept = 2 * HALO + ROWS
-    state = [tuple(narrow(x, ROWS - HALO, kept) for x in s) for s in state]
-    slopes = [tuple(narrow(x, ROWS - HALO, kept) for x in s) for s in slopes]
-    masks = [narrow(x, ROWS - HALO, kept) for x in masks]
-    advanced = two_steps(state, slopes, masks)
-    for t in range(tile_count):
-        for f in range(3):
-            new, old = narrow(advanced[t][f], HALO, ROWS), narrow(state[t][f], HALO, ROWS)
-            tiles[t, f * ROWS : (f + 1) * ROWS] = jnp.where(wets[t][ROWS : 2 * ROWS] > 0.5, new, old)
+    state = tuple(narrow(x, ROWS - HALO, kept) for x in state)
+    slopes = tuple(narrow(x, ROWS - HALO, kept) for x in slopes)
+    advanced = two_steps(state, slopes, narrow(masks, ROWS - HALO, kept))
+    wet = wets[:tile_count, ROWS : 2 * ROWS] > 0.5
+    for f in range(3):
+        new, old = narrow(advanced[f], HALO, ROWS)[:tile_count], narrow(state[f], HALO, ROWS)[:tile_count]
+        tiles[:, f * ROWS : (f + 1) * ROWS] = jnp.where(wet, new, old)
 
     for target in range(n_cols):
         outgoing[target, : 3 * ROWS] = tiles[jnp.maximum(chosen[target], 0)]

time: 33.3 us -> 32.5 us (0.976)
  Pallas kernels: 32.5 us -> 31.7 us
    pallas_call x1, Pallas kernels: 32.5 us -> 31.7 us  [step(): pl.pallas_call(functools.partial(kernel, (n_rows, n_cols)), out_shape=plt...]
where the time goes in v4:
time: 32.5 us; the launch traced here: 32.3 us
  Pallas kernels  31.7 us (98%)
  local copies, waits for them, and re-layouts  0.64 us (2%)
    pallas_call x1, Pallas kernels, step(): pl.pallas_call(functools.partial(kernel, (n_rows, n_cols)), out_shape=plt...  31.7 us

profile of v4, /device:TPU:63, one launch (start us, length us, event | category | flops | bytes accessed | tf_op | source)
XLA Modules:
  0.0 32.3 jit_solution(1543364375011967777)
XLA Ops:
  0.0 31.7 %shard_map.55 = f32[3,8,1024]{2,1,0:T(8,128)S(1)} custom-call(f32[8,1024]{1,0:T(8,128)} %depth_hbm.1, f32[2,8,1024]{2,1,0:T(8,128)} %velocity_hbm.1, f32[8,1024]{1,0:T(8,128)} %bed_hbm.1, s32[1,8]{1,0:T(1,128)} %wet_hbm.1, s32[1,8]{1,0:T(1,128)} %migration_hbm.1), custom_call_target="tpu_custom_call" | custom-call | tf_op jit(solution)/shard_map/pallas_call | solution.py:362
  31.7 0.6 %copy.7 = f32[3,8,1024]{2,1,0:T(8,128)} copy(f32[3,8,1024]{2,1,0:T(8,128)S(1)} %shard_map.55) | data formatting | bytes 196608

commit v5 on v4

--- a/solution.py
+++ b/solution.py
@@ -9,6 +9,7 @@
 
 DRY_DEPTH = 0.05
 COURANT = 0.15
+SCALE = 0.5 * COURANT
 HALO = 4
 ROWS = 8
 LANES = 128
@@ -49,11 +50,11 @@
 def fluxes(h, p, q):
     floored = jnp.maximum(h, DRY_DEPTH)
     inverse_root = lax.rsqrt(floored)
-    celerity = floored * inverse_root
+    celerity = floored * (SCALE * inverse_root)
     inverse = inverse_root * inverse_root
     u = p * inverse
     v = q * inverse
-    pressure = 0.5 * h * h
+    pressure = (0.5 * SCALE * SCALE) * h * h
     east, cross, north = p * u + pressure, q * u, q * v + pressure
     speed = jnp.abs(u) + celerity
     turned = tuple(turn(x, -1, 2) for x in (h, p, q, east, cross, speed))
@@ -87,12 +88,11 @@
     moved = []
     for f, cells in enumerate((h, p, q)):
         face, back, before = columns[f::3]
-        change = (face - jnp.where(first, before, back)) + (rows[f] - turn(rows[f], 1, 1))
-        new = cells - (0.5 * COURANT) * change
+        new = cells - ((face - jnp.where(first, before, back)) + (rows[f] - turn(rows[f], 1, 1)))
         if f:
             new = new - h * slopes[f - 1]
         if start:
-            new = 0.5 * start[f] + 0.5 * new
+            new = 0.5 * (start[f] + new)
         moved.append(new * mask)
     return moved
 
@@ -293,10 +293,11 @@
 
     masks = jnp.stack(masks)
     depth, across, along, beds = (jnp.where(masks > 0.5, jnp.stack(field), 0.0) for field in fields)
-    state = (depth, depth * across, depth * along)
+    scaled = SCALE * depth
+    state = (depth, scaled * across, scaled * along)
     slopes = (
-        (0.5 * COURANT) * (ring_next(beds) - ring_previous(beds)),
-        (0.5 * COURANT) * (turn(beds, -1, 1) - turn(beds, 1, 1)),
+        (SCALE * SCALE) * (ring_next(beds) - ring_previous(beds)),
+        (SCALE * SCALE) * (turn(beds, -1, 1) - turn(beds, 1, 1)),
     )
     wets = jnp.stack(wets)
     advanced = two_steps(state, slopes, masks)
@@ -312,7 +313,7 @@
     wet = wets[:tile_count, ROWS : 2 * ROWS] > 0.5
     for f in range(3):
         new, old = narrow(advanced[f], HALO, ROWS)[:tile_count], narrow(state[f], HALO, ROWS)[:tile_count]
-        tiles[:, f * ROWS : (f + 1) * ROWS] = jnp.where(wet, new, old)
+        tiles[:, f * ROWS : (f + 1) * ROWS] = jnp.where(wet, new, old) * (1.0 / SCALE if f else 1.0)
 
     for target in range(n_cols):
         outgoing[target, : 3 * ROWS] = tiles[jnp.maximum(chosen[target], 0)]
@@ -325,7 +326,11 @@
         remote(outgoing.at[target, slot], arrived.at[gy, slot], slot_send, slot_recv, (gx, target)).start()
         return carry
 
-    lax.fori_loop(0, gy, send_slot, 0)
+    def from_both_ends(i, carry):
+        half = i // 2
+        return send_slot(jnp.where(lax.rem(i, 2) == 0, half, gy - 1 - half), carry)
+
+    lax.fori_loop(0, gy, from_both_ends, 0)
 
     @pl.when(has_right)
     def _():

time: 32.5 us -> 32.5 us (level)
  no operation moved by 1% of the time
where the time goes in v5:
time: 32.5 us; the launch traced here: 32.3 us
  Pallas kernels  31.7 us (98%)
  local copies, waits for them, and re-layouts  0.64 us (2%)
    pallas_call x1, Pallas kernels, step(): pl.pallas_call(functools.partial(kernel, (n_rows, n_cols)), out_shape=plt...  31.7 us

profile of v5, /device:TPU:63, one launch (start us, length us, event | category | flops | bytes accessed | tf_op | source)
XLA Modules:
  0.0 32.3 jit_solution(13914812360855309572)
XLA Ops:
  0.0 31.7 %shard_map.55 = f32[3,8,1024]{2,1,0:T(8,128)S(1)} custom-call(f32[8,1024]{1,0:T(8,128)} %depth_hbm.1, f32[2,8,1024]{2,1,0:T(8,128)} %velocity_hbm.1, f32[8,1024]{1,0:T(8,128)} %bed_hbm.1, s32[1,8]{1,0:T(1,128)} %wet_hbm.1, s32[1,8]{1,0:T(1,128)} %migration_hbm.1), custom_call_target="tpu_custom_call" | custom-call | tf_op jit(solution)/shard_map/pallas_call | solution.py:367
  31.7 0.6 %copy.7 = f32[3,8,1024]{2,1,0:T(8,128)} copy(f32[3,8,1024]{2,1,0:T(8,128)S(1)} %shard_map.55) | data formatting | bytes 196608

commit v6 on v5

--- a/solution.py
+++ b/solution.py
@@ -97,7 +97,7 @@
     return moved
 
 
-def half_step(state, slopes, masks, start):
+def half_step(state, slopes, masks, start, kept=None):
     h, p, q = state
     group = GROUP if h.shape[1] > 2 * ROWS else GROUP_2
     east, cross, reach_x, north, reach_y, *turned = by_group(fluxes, group, state)
@@ -106,13 +106,13 @@
     columns = by_group(column_faces, group, here + turned + after)
     before = [jnp.concatenate([x[-1:], x[:-1]], axis=0) for x in columns[3:]]
     others = columns + before + list(slopes) + [masks] + list(start or ())
-    return by_group(update, group, [h, p, q, cross, north, reach_y] + others)
-
-
-def two_steps(state, slopes, masks):
-    for _ in range(2):
+    return by_group(update, group, [x[:kept] for x in [h, p, q, cross, north, reach_y] + others])
+
+
+def two_steps(state, slopes, masks, kept=None):
+    for step in range(2):
         middle = half_step(state, slopes, masks, None)
-        state = half_step(middle, slopes, masks, state)
+        state = half_step(middle, slopes, masks, state, kept if step else None)
     return state
 
 
@@ -309,7 +309,7 @@
     kept = 2 * HALO + ROWS
     state = tuple(narrow(x, ROWS - HALO, kept) for x in state)
     slopes = tuple(narrow(x, ROWS - HALO, kept) for x in slopes)
-    advanced = two_steps(state, slopes, narrow(masks, ROWS - HALO, kept))
+    advanced = two_steps(state, slopes, narrow(masks, ROWS - HALO, kept), tile_count)
     wet = wets[:tile_count, ROWS : 2 * ROWS] > 0.5
     for f in range(3):
         new, old = narrow(advanced[f], HALO, ROWS)[:tile_count], narrow(state[f], HALO, ROWS)[:tile_count]

time: 32.5 us -> 32.5 us (level)
  no operation moved by 1% of the time
where the time goes in v6:
time: 32.5 us; the launch traced here: 32.3 us
  Pallas kernels  31.7 us (98%)
  local copies, waits for them, and re-layouts  0.64 us (2%)
    pallas_call x1, Pallas kernels, step(): pl.pallas_call(functools.partial(kernel, (n_rows, n_cols)), out_shape=plt...  31.7 us

profile of v6, /device:TPU:63, one launch (start us, length us, event | category | flops | bytes accessed | tf_op | source)
XLA Modules:
  0.0 32.3 jit_solution(13914812360855309572)
XLA Ops:
  0.0 31.7 %shard_map.55 = f32[3,8,1024]{2,1,0:T(8,128)S(1)} custom-call(f32[8,1024]{1,0:T(8,128)} %depth_hbm.1, f32[2,8,1024]{2,1,0:T(8,128)} %velocity_hbm.1, f32[8,1024]{1,0:T(8,128)} %bed_hbm.1, s32[1,8]{1,0:T(1,128)} %wet_hbm.1, s32[1,8]{1,0:T(1,128)} %migration_hbm.1), custom_call_target="tpu_custom_call" | custom-call | tf_op jit(solution)/shard_map/pallas_call | solution.py:367
  31.7 0.6 %copy.7 = f32[3,8,1024]{2,1,0:T(8,128)} copy(f32[3,8,1024]{2,1,0:T(8,128)S(1)} %shard_map.55) | data formatting | bytes 196608
